TPU v7x, 32 devices: a whole 2x2x4 slice. The times are simulated.
32 devices in a mesh: ctx: 8 (over z, x), tp: 4 (over y, core).
Axes of the slice: x: 2, y: 2, z: 4, core: 2. Of those that a mesh axis runs over, the one named last changes fastest.
Arguments:
- tokens: bfloat16 [4096, 4096], P('ctx', 'tp'), may hold values from -16 to 16
- query_weight: bfloat16 [4096, 4096], P(None, 'tp'), may hold values from -0.09375 to 0.09375
- key_weight: bfloat16 [4096, 1024], P(None, 'tp'), may hold values from -0.09375 to 0.09375
- value_weight: bfloat16 [4096, 1024], P(None, 'tp'), may hold values from -0.09375 to 0.09375
- out_weight: bfloat16 [4096, 4096], P('tp'), may hold values from -0.09375 to 0.09375
- links: int32 [32, 16], P('ctx'), may hold values from 0 to 31, as said below
- counts: int32 [32], P('ctx'), may hold values from 1 to 16, as said below
- doc_ids: int32 [32], replicated, may hold values from 0 to 7, never falling along the last dimension, each value on 1 to 8 neighbouring positions
Outputs:
- mixed: bfloat16 [4096, 4096], P(('ctx', 'tp'))
Inputs may be any that keep to these rules, and one draw needn't show every extreme that they name: `links`: the first entry of each row is the query block itself; the entries of a row are distinct; every listed block lies within 4 ctx indices of its query block (block index // 4), and some query block of every ctx index lists a block exactly 4 indices away. `counts`: the first query block of each ctx index has 2 or more live slots, and block 0 has 16.
All inputs are finite; a program needn't handle non-finite values.
Results may differ from a plain program's by a relative error of at most 0.017.
Values may be sent and summed in bfloat16 or wider, within the bound.
A program may use at most 128 MiB of HBM per device.

v0:
```python
import functools

import jax
import jax.numpy as jnp
from jax import lax
from jax.experimental import pallas as pl
from jax.experimental.pallas import tpu as pltpu
from jax.sharding import PartitionSpec as P

HEAD_DIM = 128
BLOCK = 128
LINKS = 16
REACH = 4
CORES = 2
BF16 = jnp.bfloat16
F32 = jnp.float32
VMEM = pl.BlockSpec(memory_space=pltpu.VMEM)
SMEM = pl.BlockSpec(memory_space=pltpu.SMEM)
ANY = pl.BlockSpec(memory_space=pl.ANY)
GRANT = 56 * 1024 * 1024


def gather_kernel(
    tp, ctx, hops, tokens_ref, query_weight_ref, key_weight_ref, value_weight_ref,
    query_ref, source_ref, token_buf, query_weight, key_weight, value_weight, stage,
    load_sems, weight_sems, store_sems, y_send, y_recv, m_send, m_recv,
    x_send, x_recv, full_send, full_recv, half_send, half_recv, k_send, k_recv
):
    blocks = tokens_ref.shape[0] // BLOCK
    across = tp // CORES
    depth = tokens_ref.shape[1]
    pairs = ctx // 2
    me = lax.axis_index("tp")
    chip, core = lax.div(me, CORES), lax.rem(me, CORES)
    mate = chip * CORES + 1 - core
    here = lax.axis_index("ctx")
    pair, side = lax.div(here, 2), lax.rem(here, 2)
    beside = pair * 2 + 1 - side
    ways = (1, -1)

    def exists(offset):
        return (pair + offset >= 0) & (pair + offset < pairs)

    def needed(offset, holder, reader):
        distance = 2 * offset + holder - reader
        return (distance <= REACH) & (distance >= -REACH)

    def slot(offset, holder):
        return (offset + hops) * 2 + holder

    def peer(step):
        return lax.rem(chip + step, across) * CORES + core

    def rows_of(block):
        return pl.ds(pl.multiple_of(block * BLOCK, BLOCK), BLOCK)

    def load(block):
        return pltpu.make_async_copy(
            tokens_ref.at[rows_of(block)], token_buf.at[me, block], load_sems.at[block]
        )

    def y_copy(block, step):
        return pltpu.make_async_remote_copy(
            src_ref=tokens_ref.at[rows_of(block)],
            dst_ref=token_buf.at[me, block],
            send_sem=y_send.at[step - 1, block],
            recv_sem=y_recv.at[step - 1, block],
            device_id={"tp": peer(step)},
        )

    def m_copy(block, step):
        owner = peer(across - step)
        if step == 0:
            source, owner = tokens_ref.at[rows_of(block)], me
        else:
            source = token_buf.at[owner, block]
        return pltpu.make_async_remote_copy(
            src_ref=source,
            dst_ref=token_buf.at[owner, block],
            send_sem=m_send.at[step, block],
            recv_sem=m_recv.at[step, block],
            device_id={"tp": mate},
        )

    weight_copies = [
        pltpu.make_async_copy(key_weight_ref, key_weight, weight_sems.at[0]),
        pltpu.make_async_copy(value_weight_ref, value_weight, weight_sems.at[1]),
        pltpu.make_async_copy(query_weight_ref, query_weight, weight_sems.at[2]),
    ]

    def begin(block, carry):
        load(block).start()
        return carry

    lax.fori_loop(0, blocks, begin, 0)
    for copy in weight_copies:
        copy.start()

    barrier = pltpu.get_barrier_semaphore()
    pl.semaphore_signal(barrier, inc=1, device_id={"tp": mate})
    for step in range(1, across):
        pl.semaphore_signal(barrier, inc=1, device_id={"tp": peer(step)})
    pl.semaphore_signal(barrier, inc=1, device_id={"ctx": beside})
    for way in ways:

        @pl.when(exists(way))
        def _(way=way):
            pl.semaphore_signal(barrier, inc=1, device_id={"ctx": here + 2 * way})

    expected = across + 1 + exists(1).astype(jnp.int32) + exists(-1).astype(jnp.int32)
    pl.semaphore_wait(barrier, expected)

    def push(block, carry):
        for step in range(1, across):
            y_copy(block, step).start()
        m_copy(block, 0).start()
        return carry

    lax.fori_loop(0, blocks, push, 0)

    def store(block):
        return pltpu.make_async_copy(
            stage.at[block], source_ref.at[slot(0, side), block], store_sems.at[block]
        )

    def x_copy(block):
        return pltpu.make_async_remote_copy(
            src_ref=stage.at[block],
            dst_ref=source_ref.at[slot(0, side), block],
            send_sem=x_send.at[block],
            recv_sem=x_recv.at[block],
            device_id={"ctx": beside},
        )

    def full_copy(block, way, hop):
        source = stage.at[block] if hop == 1 else source_ref.at[slot(-way * (hop - 1), side), block]
        return pltpu.make_async_remote_copy(
            src_ref=source,
            dst_ref=source_ref.at[slot(-way * hop, side), block],
            send_sem=full_send.at[ways.index(way), hop - 1, block],
            recv_sem=full_recv.at[ways.index(way), hop - 1, block],
            device_id={"ctx": here + 2 * way},
        )

    def half_copy(block, way, hop):
        return pltpu.make_async_remote_copy(
            src_ref=source_ref.at[slot(-way * (hop - 1), 1 - side), block, 1],
            dst_ref=source_ref.at[slot(-way * hop, 1 - side), block, 1],
            send_sem=half_send.at[ways.index(way), hop - 1, block],
            recv_sem=half_recv.at[ways.index(way), hop - 1, block],
            device_id={"ctx": here + 2 * way},
        )

    def k_copy(block, way, hop):
        return pltpu.make_async_remote_copy(
            src_ref=source_ref.at[slot(-way * hop, side), block, 0],
            dst_ref=source_ref.at[slot(-way * hop, side), block, 0],
            send_sem=k_send.at[ways.index(way), hop - 1, block],
            recv_sem=k_recv.at[ways.index(way), hop - 1, block],
            device_id={"ctx": beside},
        )

    def full_sent(way, hop):
        return exists(way) & exists(-way * (hop - 1))

    def full_due(way, hop):
        return exists(-way * hop)

    def half_sent(way, hop):
        return full_sent(way, hop) & needed(-way * hop, 1 - side, side)

    def half_due(way, hop):
        return full_due(way, hop) & needed(-way * hop, 1 - side, side)

    def k_sent(way, hop):
        return full_due(way, hop) & needed(-way * hop, side, 1 - side)

    def k_due(way, hop):
        return full_due(way, hop) & needed(-way * hop, 1 - side, side)

    def k_received(block, way, hop):
        return pltpu.make_async_remote_copy(
            src_ref=source_ref.at[slot(-way * hop, 1 - side), block, 0],
            dst_ref=source_ref.at[slot(-way * hop, 1 - side), block, 0],
            send_sem=k_send.at[ways.index(way), hop - 1, block],
            recv_sem=k_recv.at[ways.index(way), hop - 1, block],
            device_id={"ctx": beside},
        )

    def multiply(block, weight, lanes):
        return sum(
            jnp.dot(
                token_buf[part, block],
                weight[part * depth : (part + 1) * depth, lanes],
                preferred_element_type=F32,
            )
            for part in range(tp)
        ).astype(BF16)

    def make(block):
        for step in range(1, across):
            y_copy_in(block, step).wait_recv()
            m_copy(block, step).start()
        load(block).wait()
        for step in range(across):
            m_copy_in(block, step).wait_recv()

        @pl.when(block == 0)
        def _():
            weight_copies[0].wait()
            weight_copies[1].wait()

        stage[block, 0] = multiply(block, key_weight, slice(None))
        stage[block, 1] = multiply(block, value_weight, slice(None))
        for way in ways:

            @pl.when(full_sent(way, 1))
            def _(way=way):
                full_copy(block, way, 1).start()

        x_copy(block).start()
        store(block).start()

    def y_copy_in(block, step):
        owner = peer(across - step)
        return pltpu.make_async_remote_copy(
            src_ref=tokens_ref.at[rows_of(block)],
            dst_ref=token_buf.at[owner, block],
            send_sem=y_send.at[step - 1, block],
            recv_sem=y_recv.at[step - 1, block],
            device_id={"tp": peer(step)},
        )

    def m_copy_in(block, step):
        owner = lax.rem(chip + across - step, across) * CORES + 1 - core
        return pltpu.make_async_remote_copy(
            src_ref=tokens_ref.at[rows_of(block)],
            dst_ref=token_buf.at[owner, block],
            send_sem=m_send.at[step, block],
            recv_sem=m_recv.at[step, block],
            device_id={"tp": mate},
        )

    def x_copy_in(block):
        return pltpu.make_async_remote_copy(
            src_ref=stage.at[block],
            dst_ref=source_ref.at[slot(0, 1 - side), block],
            send_sem=x_send.at[block],
            recv_sem=x_recv.at[block],
            device_id={"ctx": beside},
        )

    def relay(block, lag):
        if lag == 1:
            x_copy_in(block).wait_recv()
            for way in ways:

                @pl.when(half_sent(way, 1))
                def _(way=way):
                    half_copy(block, way, 1).start()

        for way in ways:
            if lag <= hops:

                @pl.when(full_due(way, lag))
                def _(way=way):
                    full_copy(block, way, lag).wait_recv()

                if lag < hops:

                    @pl.when(full_sent(way, lag + 1))
                    def _(way=way):
                        full_copy(block, way, lag + 1).start()

                @pl.when(k_sent(way, lag))
                def _(way=way):
                    k_copy(block, way, lag).start()

            if lag > 1:

                @pl.when(half_due(way, lag - 1))
                def _(way=way):
                    half_copy(block, way, lag - 1).wait_recv()

                if lag <= hops:

                    @pl.when(half_sent(way, lag))
                    def _(way=way):
                        half_copy(block, way, lag).start()

    def step_of(step, carry):
        @pl.when(step < blocks)
        def _():
            make(step)

        for lag in range(1, hops + 2):

            @pl.when((step >= lag) & (step - lag < blocks))
            def _(lag=lag):
                relay(step - lag, lag)

        @pl.when(step == 0)
        def _():
            weight_copies[2].wait()

        @pl.when(step < blocks)
        def _():
            width = query_ref.shape[1]
            wide = min(512, width)
            for start in range(0, width, wide):
                lanes = slice(start, start + wide)
                query_ref[rows_of(step), lanes] = multiply(step, query_weight, lanes)

        return carry

    lax.fori_loop(0, blocks + hops + 1, step_of, 0)

    def drain(block, carry):
        for step in range(1, across):
            y_copy(block, step).wait_send()
        for step in range(across):
            m_copy(block, step).wait_send()
        store(block).wait()
        x_copy(block).wait_send()
        for way in ways:
            for hop in range(1, hops + 1):

                @pl.when(k_due(way, hop))
                def _(way=way, hop=hop):
                    k_received(block, way, hop).wait_recv()

                @pl.when(full_sent(way, hop))
                def _(way=way, hop=hop):
                    full_copy(block, way, hop).wait_send()

                @pl.when(half_sent(way, hop))
                def _(way=way, hop=hop):
                    half_copy(block, way, hop).wait_send()

                @pl.when(k_sent(way, hop))
                def _(way=way, hop=hop):
                    k_copy(block, way, hop).wait_send()

        return carry

    lax.fori_loop(0, blocks, drain, 0)


def gather(tokens, query_weight, key_weight, value_weight):
    tp, ctx = lax.axis_size("tp"), lax.axis_size("ctx")
    across = tp // CORES
    hops = (REACH + 1) // 2
    row_count, depth = tokens.shape
    blocks = row_count // BLOCK
    query_width, key_width = query_weight.shape[1], key_weight.shape[1]
    slots = (2 * hops + 1) * 2
    dma = pltpu.SemaphoreType.DMA
    return pl.pallas_call(
        functools.partial(gather_kernel, tp, ctx, hops),
        out_shape=(
            jax.ShapeDtypeStruct((row_count, query_width), BF16),
            jax.ShapeDtypeStruct((slots, blocks, 2, BLOCK, key_width), BF16),
        ),
        in_specs=[ANY] * 4,
        out_specs=(VMEM, ANY),
        scratch_shapes=[
            pltpu.VMEM((tp, blocks, BLOCK, depth), BF16),
            pltpu.VMEM(query_weight.shape, BF16),
            pltpu.VMEM(key_weight.shape, BF16),
            pltpu.VMEM(value_weight.shape, BF16),
            pltpu.VMEM((blocks, 2, BLOCK, key_width), BF16),
            dma((blocks,)),
            dma((3,)),
            dma((blocks,)),
            dma((max(across - 1, 1), blocks)),
            dma((max(across - 1, 1), blocks)),
            dma((across, blocks)),
            dma((across, blocks)),
            dma((blocks,)),
            dma((blocks,)),
            dma((2, hops, blocks)),
            dma((2, hops, blocks)),
            dma((2, hops, blocks)),
            dma((2, hops, blocks)),
            dma((2, hops, blocks)),
            dma((2, hops, blocks)),
        ],
        compiler_params=pltpu.CompilerParams(
            collective_id=0, has_side_effects=True, vmem_limit_bytes=GRANT
        ),
        cost_estimate=pl.CostEstimate(
            flops=2 * row_count * depth * tp * (query_width + 2 * key_width),
            bytes_accessed=1 << 24,
            transcendentals=0,
        ),
    )(tokens, query_weight, key_weight, value_weight)


def finish_kernel(
    tp, chunks, wide, group, hops, links_ref, counts_ref, docs_ref, query_ref, source_ref,
    weight_ref, out_ref, source_buf, weight_buf, score_buf, attended, part_buf, own_buf,
    mate_send, mate_recv, far_send, far_recv, source_sem, weight_sems, mate_send_sems,
    mate_recv_sems, far_send_sems, far_recv_sems
):
    row_count = query_ref.shape[0]
    blocks = row_count // BLOCK
    kv_heads = source_ref.shape[3] // HEAD_DIM
    rows = row_count // tp
    tall = rows * CORES
    across = tp // CORES
    me = lax.axis_index("tp")
    chip, core = lax.div(me, CORES), lax.rem(me, CORES)
    mate = chip * CORES + 1 - core
    here = lax.axis_index("ctx")
    first = here * blocks
    anchor = (lax.div(here, 2) - hops) * 2 * blocks

    source_copy = pltpu.make_async_copy(source_ref, source_buf, source_sem.at[0])
    source_copy.start()

    def weight_copy(index):
        columns = pl.ds(pl.multiple_of(index * wide, wide), wide)
        return pltpu.make_async_copy(
            weight_ref.at[:, columns], weight_buf.at[index], weight_sems.at[index]
        )

    def start_weight(index, carry):
        weight_copy(index).start()
        return carry

    lax.fori_loop(0, chunks, start_weight, 0)

    barrier = pltpu.get_barrier_semaphore()
    pl.semaphore_signal(barrier, inc=1, device_id={"tp": mate})
    for step in range(1, across):
        other = lax.rem(chip + step, across) * CORES + core
        pl.semaphore_signal(barrier, inc=1, device_id={"tp": other})
    pl.semaphore_wait(barrier, across)
    source_copy.wait()

    scale = HEAD_DIM ** (-0.5) * 1.4426950408889634
    pair = 2 * BLOCK
    height = group * BLOCK
    token = lax.rem(lax.broadcasted_iota(jnp.int32, (height, pair), 0), BLOCK)
    column = lax.broadcasted_iota(jnp.int32, (height, pair), 1)
    row_column = lax.broadcasted_iota(jnp.int32, (1, pair), 1)

    def attend(block):
        mine = first + block
        doc = docs_ref[mine]
        live = counts_ref[block]
        places, biases = [], []
        for slot in range(LINKS):
            listed = links_ref[block, slot]
            seen = (slot < live) & ((listed <= mine) | (docs_ref[listed] != doc))
            places.append(jnp.clip(listed - anchor, 0, source_ref.shape[0] - 1))
            biases.append(jnp.where(seen, 0.0, -1e30))
        at = pl.ds(pl.multiple_of(block * BLOCK, BLOCK), BLOCK)

        def of_head(head, carry):
            lanes = pl.ds(pl.multiple_of(head * HEAD_DIM, HEAD_DIM), HEAD_DIM)

            def lanes_of(member):
                start = pl.multiple_of((head * group + member) * HEAD_DIM, HEAD_DIM)
                return pl.ds(start, HEAD_DIM)

            def two(index, kind):
                return jnp.concatenate(
                    [source_buf[places[2 * index + i], kind, :, lanes] for i in range(2)], axis=0
                )

            query = jnp.concatenate(
                [query_ref[at, lanes_of(member)] for member in range(group)], axis=0
            )
            top = None
            for index in range(LINKS // 2):
                scores = lax.dot_general(
                    query, two(index, 0), (((1,), (1,)), ((), ())), preferred_element_type=F32
                )
                bias = jnp.where(row_column < BLOCK, biases[2 * index], biases[2 * index + 1])
                scores = scores * scale + bias
                if index == 0:
                    scores = jnp.where((column >= BLOCK) | (column <= token), scores, -1e30)
                score_buf[index] = scores
                both = jnp.maximum(scores[:, :BLOCK], scores[:, BLOCK:])
                top = both if top is None else jnp.maximum(top, both)
            top = jnp.max(top, axis=1, keepdims=True)
            total, result = None, None
            for index in range(LINKS // 2):
                powers = jnp.exp2(score_buf[index] - top)
                both = powers[:, :BLOCK] + powers[:, BLOCK:]
                total = both if total is None else total + both
                term = jnp.dot(powers.astype(BF16), two(index, 1), preferred_element_type=F32)
                result = term if result is None else result + term
            total = jnp.sum(total, axis=1, keepdims=True)
            result = (result / total).astype(BF16)
            for member in range(group):
                attended[at, lanes_of(member)] = result[member * BLOCK : (member + 1) * BLOCK]
            return carry

        lax.fori_loop(0, kv_heads, of_head, 0)

    def mate_copy(index, step):
        return pltpu.make_async_remote_copy(
            src_ref=mate_send.at[index, step],
            dst_ref=mate_recv.at[index, step],
            send_sem=mate_send_sems.at[index, step],
            recv_sem=mate_recv_sems.at[index, step],
            device_id={"tp": mate},
        )

    def far_copy(index, step):
        other = lax.rem(chip + step, across) * CORES + core
        return pltpu.make_async_remote_copy(
            src_ref=far_send.at[index, step - 1],
            dst_ref=far_recv.at[index, step - 1],
            send_sem=far_send_sems.at[index, step - 1],
            recv_sem=far_recv_sems.at[index, step - 1],
            device_id={"tp": other},
        )

    def rows_of(which):
        return pl.ds(pl.multiple_of(which * rows, rows), rows)

    def turn_of(turn, carry):
        step = lax.rem(turn + 1, across)
        target = lax.rem(chip + step, across)
        per_chip = tall // BLOCK

        def attend_one(index, carry):
            attend(target * per_chip + index)
            return carry

        lax.fori_loop(0, per_chip, attend_one, 0)
        at = pl.ds(pl.multiple_of(target * tall, tall), tall)

        def multiply(index):
            @pl.when(turn == 0)
            def _():
                weight_copy(index).wait()

            part_buf[lax.rem(index, 2)] = jnp.dot(
                attended[at], weight_buf[index], preferred_element_type=F32
            )
            mate_send[index, step] = part_buf[lax.rem(index, 2), rows_of(1 - core)].astype(BF16)
            mate_copy(index, step).start()

        def combine(index):
            mate_copy(index, step).wait_recv()
            total = part_buf[lax.rem(index, 2), rows_of(core)] + mate_recv[index, step].astype(F32)

            @pl.when(step == 0)
            def _():
                own_buf[index] = total

            @pl.when(step > 0)
            def _():
                far_send[index, step - 1] = total.astype(BF16)
                far_copy(index, step).start()

        multiply(0)

        def middle(index, carry):
            multiply(index)
            combine(index - 1)
            return carry

        lax.fori_loop(1, chunks, middle, 0)
        combine(chunks - 1)
        return carry

    lax.fori_loop(0, across, turn_of, 0)

    def close(index, carry):
        total = own_buf[index]
        for step in range(1, across):
            far_copy(index, step).wait_recv()
            total = total + far_recv[index, step - 1].astype(F32)
        columns = pl.ds(pl.multiple_of(index * wide, wide), wide)
        out_ref[:, columns] = total.astype(BF16)
        return carry

    lax.fori_loop(0, chunks, close, 0)

    def drain(index, carry):
        for step in range(across):
            mate_copy(index, step).wait_send()
        for step in range(1, across):
            far_copy(index, step).wait_send()
        return carry

    lax.fori_loop(0, chunks, drain, 0)


def finish(links, counts, doc_ids, query, source, out_weight):
    tp = lax.axis_size("tp")
    across = tp // CORES
    hops = (REACH + 1) // 2
    row_count, depth = query.shape
    width = out_weight.shape[1]
    group = depth // source.shape[3]
    rows = row_count // tp
    wide = min(512, width)
    chunks = width // wide
    dma = pltpu.SemaphoreType.DMA
    return pl.pallas_call(
        functools.partial(finish_kernel, tp, chunks, wide, group, hops),
        out_shape=jax.ShapeDtypeStruct((rows, width), BF16),
        in_specs=[SMEM, SMEM, SMEM, VMEM, ANY, ANY],
        out_specs=VMEM,
        scratch_shapes=[
            pltpu.VMEM(source.shape, BF16),
            pltpu.VMEM((chunks, depth, wide), BF16),
            pltpu.VMEM((LINKS // 2, group * BLOCK, 2 * BLOCK), F32),
            pltpu.VMEM((row_count, depth), BF16),
            pltpu.VMEM((2, rows * CORES, wide), F32),
            pltpu.VMEM((chunks, rows, wide), F32),
            pltpu.VMEM((chunks, across, rows, wide), BF16),
            pltpu.VMEM((chunks, across, rows, wide), BF16),
            pltpu.VMEM((chunks, max(across - 1, 1), rows, wide), BF16),
            pltpu.VMEM((chunks, max(across - 1, 1), rows, wide), BF16),
            dma((1,)),
            dma((chunks,)),
            dma((chunks, across)),
            dma((chunks, across)),
            dma((chunks, max(across - 1, 1))),
            dma((chunks, max(across - 1, 1))),
        ],
        compiler_params=pltpu.CompilerParams(
            collective_id=1, has_side_effects=True, vmem_limit_bytes=GRANT
        ),
        cost_estimate=pl.CostEstimate(
            flops=2 * row_count * depth * (width + 2 * LINKS * BLOCK),
            bytes_accessed=1 << 24,
            transcendentals=0,
        ),
    )(links, counts, doc_ids, query, source, out_weight)


def local(tokens, query_weight, key_weight, value_weight, out_weight, links, counts, doc_ids):
    query, source = gather(tokens, query_weight, key_weight, value_weight)
    source = source.reshape((-1,) + source.shape[2:])
    return finish(links, counts, doc_ids, query, source, out_weight)


def solution(mesh):
    placed = (
        P("ctx", "tp"),
        P(None, "tp"),
        P(None, "tp"),
        P(None, "tp"),
        P("tp", None),
        P("ctx", None),
        P("ctx"),
        P(),
    )
    return jax.shard_map(
        local, mesh=mesh, in_specs=placed, out_specs=P(("ctx", "tp"), None), check_vma=False
    )
```

profile of v0, /device:TPU:6, one launch (start us, length us, event | category | flops | bytes accessed | tf_op | source)
XLA Modules:
  0.0 98.9 jit_solution(12545524177961118273)
XLA Ops:
  0.0 52.8 %shard_map.82 = (bf16[512,1024]{1,0:T(8,128)(2,1)}, bf16[10,4,2,128,256]{4,3,2,1,0:T(8,128)(2,1)}) custom-call(bf16[512,1024]{1,0:T(8,128)(2,1)} %tokens_ref.1, bf16[4096,1024]{1,0:T(8,128)(2,1)} %query_weight_ref.1, bf16[4096,256]{1,0:T(8,128)(2,1)} %key_weight_ref.1, bf16[4096,256]{1,0:T(8,128)(2,1)} %value_weight_ref.1), custom_call_target="tpu_custom_call" | custom-call | flops 6442450944 | bytes 16777216 | tf_op jit(solution)/shard_map/pallas_call | solution.py:358
  52.9 43.8 %shard_map.83 = bf16[128,4096]{1,0:T(8,128)(2,1)} custom-call(s32[4,16]{1,0:T(4,128)} %links_ref.1, s32[4]{0:T(128)} %counts_ref.1, s32[32]{0:T(128)} %docs_ref.1, bf16[512,1024]{1,0:T(8,128)(2,1)} %get-tuple-element.7.query_ref, bf16[40,2,128,256]{3,2,1,0:T(8,128)(2,1)} %bitcast.1, bf16[1024,4096]{1,0:T(8,128)(2,1)} %weight_ref.1), custom_call_target="tpu_custom_call" | custom-call | flops 8589934592 | bytes 16777216 | tf_op jit(solution)/shard_map/pallas_call | solution.py:606
  96.6 2.3 %copy.10 = bf16[128,4096]{1,0:T(8,128)(2,1)} copy(bf16[128,4096]{1,0:T(8,128)(2,1)} %shard_map.83) | data formatting | bytes 2097152
where the time goes:
time: 100 us; the launch traced here: 98.9 us
  Pallas kernels  96.6 us (97%)
  local copies, waits for them, and re-layouts  2.29 us (2%)
    pallas_call x1, Pallas kernels, gather(): pl.pallas_call(functools.partial(gather_kernel, tp, ctx, hops), out_shape...  52.8 us
    pallas_call x1, Pallas kernels, finish(): pl.pallas_call(functools.partial(finish_kernel, tp, chunks, wide, group,...  43.8 us
    unnamed x1, local copies, waits for them, and re-layouts  2.29 us

commit v1 on v0

--- a/solution.py
+++ b/solution.py
@@ -457,48 +457,58 @@
             biases.append(jnp.where(seen, 0.0, -1e30))
         at = pl.ds(pl.multiple_of(block * BLOCK, BLOCK), BLOCK)
 
-        def of_head(head, carry):
-            lanes = pl.ds(pl.multiple_of(head * HEAD_DIM, HEAD_DIM), HEAD_DIM)
-
-            def lanes_of(member):
-                start = pl.multiple_of((head * group + member) * HEAD_DIM, HEAD_DIM)
-                return pl.ds(start, HEAD_DIM)
-
-            def two(index, kind):
-                return jnp.concatenate(
-                    [source_buf[places[2 * index + i], kind, :, lanes] for i in range(2)], axis=0
+        def lanes_of(member):
+            return slice(member * HEAD_DIM, (member + 1) * HEAD_DIM)
+
+        def two(index, kind, head):
+            return jnp.concatenate(
+                [
+                    source_buf[places[2 * index + i], kind, :, lanes_of(head)]
+                    for i in range(2)
+                ],
+                axis=0,
+            )
+
+        def first_pass(query, head, index):
+            scores = lax.dot_general(
+                query, two(index, 0, head), (((1,), (1,)), ((), ())), preferred_element_type=F32
+            )
+            bias = jnp.where(row_column < BLOCK, biases[2 * index], biases[2 * index + 1])
+            scores = scores * scale + bias
+            if index == 0:
+                scores = jnp.where((column >= BLOCK) | (column <= token), scores, -1e30)
+            score_buf[head % 2, index] = scores
+            return jnp.maximum(scores[:, :BLOCK], scores[:, BLOCK:])
+
+        def second_pass(top, head, index):
+            powers = jnp.exp2(score_buf[head % 2, index] - top)
+            term = jnp.dot(powers.astype(BF16), two(index, 1, head), preferred_element_type=F32)
+            return powers[:, :BLOCK] + powers[:, BLOCK:], term
+
+        top = None
+        for head in range(kv_heads + 1):
+            best, total, result = None, None, None
+            if head < kv_heads:
+                query = jnp.concatenate(
+                    [query_ref[at, lanes_of(head * group + member)] for member in range(group)],
+                    axis=0,
                 )
-
-            query = jnp.concatenate(
-                [query_ref[at, lanes_of(member)] for member in range(group)], axis=0
-            )
-            top = None
             for index in range(LINKS // 2):
-                scores = lax.dot_general(
-                    query, two(index, 0), (((1,), (1,)), ((), ())), preferred_element_type=F32
-                )
-                bias = jnp.where(row_column < BLOCK, biases[2 * index], biases[2 * index + 1])
-                scores = scores * scale + bias
-                if index == 0:
-                    scores = jnp.where((column >= BLOCK) | (column <= token), scores, -1e30)
-                score_buf[index] = scores
-                both = jnp.maximum(scores[:, :BLOCK], scores[:, BLOCK:])
-                top = both if top is None else jnp.maximum(top, both)
-            top = jnp.max(top, axis=1, keepdims=True)
-            total, result = None, None
-            for index in range(LINKS // 2):
-                powers = jnp.exp2(score_buf[index] - top)
-                both = powers[:, :BLOCK] + powers[:, BLOCK:]
-                total = both if total is None else total + both
-                term = jnp.dot(powers.astype(BF16), two(index, 1), preferred_element_type=F32)
-                result = term if result is None else result + term
-            total = jnp.sum(total, axis=1, keepdims=True)
-            result = (result / total).astype(BF16)
-            for member in range(group):
-                attended[at, lanes_of(member)] = result[member * BLOCK : (member + 1) * BLOCK]
-            return carry
-
-        lax.fori_loop(0, kv_heads, of_head, 0)
+                if head < kv_heads:
+                    both = first_pass(query, head, index)
+                    best = both if best is None else jnp.maximum(best, both)
+                if head > 0:
+                    both, term = second_pass(top, head - 1, index)
+                    total = both if total is None else total + both
+                    result = term if result is None else result + term
+            if head > 0:
+                result = (result / jnp.sum(total, axis=1, keepdims=True)).astype(BF16)
+                for member in range(group):
+                    attended[at, lanes_of((head - 1) * group + member)] = result[
+                        member * BLOCK : (member + 1) * BLOCK
+                    ]
+            if head < kv_heads:
+                top = jnp.max(best, axis=1, keepdims=True)
 
     def mate_copy(index, step):
         return pltpu.make_async_remote_copy(
@@ -611,7 +621,7 @@
         scratch_shapes=[
             pltpu.VMEM(source.shape, BF16),
             pltpu.VMEM((chunks, depth, wide), BF16),
-            pltpu.VMEM((LINKS // 2, group * BLOCK, 2 * BLOCK), F32),
+            pltpu.VMEM((2, LINKS // 2, group * BLOCK, 2 * BLOCK), F32),
             pltpu.VMEM((row_count, depth), BF16),
             pltpu.VMEM((2, rows * CORES, wide), F32),
             pltpu.VMEM((chunks, rows, wide), F32),

time: 100 us -> 94.7 us (0.947)
  Pallas kernels: 96.6 us -> 92.3 us
    pallas_call x1, Pallas kernels: 43.8 us -> 39.4 us  [finish(): pl.pallas_call(functools.partial(finish_kernel, tp, chunks, wide, group,...]
where the time goes in v1:
time: 94.7 us; the launch traced here: 94.6 us
  Pallas kernels  92.3 us (97%)
  local copies, waits for them, and re-layouts  2.29 us (2%)
    pallas_call x1, Pallas kernels, gather(): pl.pallas_call(functools.partial(gather_kernel, tp, ctx, hops), out_shape...  52.8 us
    pallas_call x1, Pallas kernels, finish(): pl.pallas_call(functools.partial(finish_kernel, tp, chunks, wide, group,...  39.4 us
    unnamed x1, local copies, waits for them, and re-layouts  2.29 us

profile of v1, /device:TPU:6, one launch (start us, length us, event | category | flops | bytes accessed | tf_op | source)
XLA Modules:
  0.0 94.6 jit_solution(13079450179567472198)
XLA Ops:
  0.0 52.8 %shard_map.82 = (bf16[512,1024]{1,0:T(8,128)(2,1)}, bf16[10,4,2,128,256]{4,3,2,1,0:T(8,128)(2,1)}) custom-call(bf16[512,1024]{1,0:T(8,128)(2,1)} %tokens_ref.1, bf16[4096,1024]{1,0:T(8,128)(2,1)} %query_weight_ref.1, bf16[4096,256]{1,0:T(8,128)(2,1)} %key_weight_ref.1, bf16[4096,256]{1,0:T(8,128)(2,1)} %value_weight_ref.1), custom_call_target="tpu_custom_call" | custom-call | flops 6442450944 | bytes 16777216 | tf_op jit(solution)/shard_map/pallas_call | solution.py:358
  52.9 39.4 %shard_map.83 = bf16[128,4096]{1,0:T(8,128)(2,1)} custom-call(s32[4,16]{1,0:T(4,128)} %links_ref.1, s32[4]{0:T(128)} %counts_ref.1, s32[32]{0:T(128)} %docs_ref.1, bf16[512,1024]{1,0:T(8,128)(2,1)} %get-tuple-element.7.query_ref, bf16[40,2,128,256]{3,2,1,0:T(8,128)(2,1)} %bitcast.1, bf16[1024,4096]{1,0:T(8,128)(2,1)} %weight_ref.1), custom_call_target="tpu_custom_call" | custom-call | flops 8589934592 | bytes 16777216 | tf_op jit(solution)/shard_map/pallas_call | solution.py:616
  92.3 2.3 %copy.10 = bf16[128,4096]{1,0:T(8,128)(2,1)} copy(bf16[128,4096]{1,0:T(8,128)(2,1)} %shard_map.83) | data formatting | bytes 2097152

commit v2 on v1

--- a/solution.py
+++ b/solution.py
@@ -474,7 +474,7 @@
                 query, two(index, 0, head), (((1,), (1,)), ((), ())), preferred_element_type=F32
             )
             bias = jnp.where(row_column < BLOCK, biases[2 * index], biases[2 * index + 1])
-            scores = scores * scale + bias
+            scores = scores + bias
             if index == 0:
                 scores = jnp.where((column >= BLOCK) | (column <= token), scores, -1e30)
             score_buf[head % 2, index] = scores
@@ -493,6 +493,7 @@
                     [query_ref[at, lanes_of(head * group + member)] for member in range(group)],
                     axis=0,
                 )
+                query = (query.astype(F32) * scale).astype(BF16)
             for index in range(LINKS // 2):
                 if head < kv_heads:
                     both = first_pass(query, head, index)

time: 94.7 us -> 94.7 us (level)
  no operation moved by 1% of the time
where the time goes in v2:
time: 94.7 us; the launch traced here: 94.5 us
  Pallas kernels  92.2 us (97%)
  local copies, waits for them, and re-layouts  2.29 us (2%)
    pallas_call x1, Pallas kernels, gather(): pl.pallas_call(functools.partial(gather_kernel, tp, ctx, hops), out_shape...  52.8 us
    pallas_call x1, Pallas kernels, finish(): pl.pallas_call(functools.partial(finish_kernel, tp, chunks, wide, group,...  39.4 us
    unnamed x1, local copies, waits for them, and re-layouts  2.29 us

profile of v2, /device:TPU:6, one launch (start us, length us, event | category | flops | bytes accessed | tf_op | source)
XLA Modules:
  0.0 94.5 jit_solution(17543155226077147659)
XLA Ops:
  0.0 52.8 %shard_map.82 = (bf16[512,1024]{1,0:T(8,128)(2,1)}, bf16[10,4,2,128,256]{4,3,2,1,0:T(8,128)(2,1)}) custom-call(bf16[512,1024]{1,0:T(8,128)(2,1)} %tokens_ref.1, bf16[4096,1024]{1,0:T(8,128)(2,1)} %query_weight_ref.1, bf16[4096,256]{1,0:T(8,128)(2,1)} %key_weight_ref.1, bf16[4096,256]{1,0:T(8,128)(2,1)} %value_weight_ref.1), custom_call_target="tpu_custom_call" | custom-call | flops 6442450944 | bytes 16777216 | tf_op jit(solution)/shard_map/pallas_call | solution.py:358
  52.9 39.4 %shard_map.83 = bf16[128,4096]{1,0:T(8,128)(2,1)} custom-call(s32[4,16]{1,0:T(4,128)} %links_ref.1, s32[4]{0:T(128)} %counts_ref.1, s32[32]{0:T(128)} %docs_ref.1, bf16[512,1024]{1,0:T(8,128)(2,1)} %get-tuple-element.7.query_ref, bf16[40,2,128,256]{3,2,1,0:T(8,128)(2,1)} %bitcast.1, bf16[1024,4096]{1,0:T(8,128)(2,1)} %weight_ref.1), custom_call_target="tpu_custom_call" | custom-call | flops 8589934592 | bytes 16777216 | tf_op jit(solution)/shard_map/pallas_call | solution.py:617
  92.3 2.3 %copy.10 = bf16[128,4096]{1,0:T(8,128)(2,1)} copy(bf16[128,4096]{1,0:T(8,128)(2,1)} %shard_map.83) | data formatting | bytes 2097152
